TPU v7x, 128 devices: a whole 4x4x4 slice. The times are simulated.
128 devices in a mesh: dp: 32 (over x, z_lo, y), ctx: 4 (over z_hi, core).
Axes of the slice: x: 4, y: 4, z: 4 (z_hi: 2, z_lo: 2; z = z_hi * 2 + z_lo), core: 2. Of those that a mesh axis runs over, the one named last changes fastest.
Arguments:
- tokens: bfloat16 [32, 2048, 576], P('dp', 'ctx'), may hold values from -6 to 6
- cotangent: bfloat16 [32, 2048, 576], P('dp', 'ctx'), may hold values from -6 to 6
- gain_attn: bfloat16 [576], P('dp'), may hold values from 0.099609375 to 1.8984375
- gain_mlp: bfloat16 [576], P('dp'), may hold values from 0.099609375 to 1.8984375
- w_query: bfloat16 [576, 576], P('dp', 'ctx'), may hold values from -0.25 to 0.25
- w_key: bfloat16 [576, 192], P('dp', 'ctx'), may hold values from -0.25 to 0.25
- w_value: bfloat16 [576, 192], P('dp', 'ctx'), may hold values from -0.25 to 0.25
- w_out: bfloat16 [576, 576], P('dp', 'ctx'), may hold values from -3 to 3
- w_gate: bfloat16 [576, 1536], P('dp', 'ctx'), may hold values from -0.25 to 0.25
- w_up: bfloat16 [576, 1536], P('dp', 'ctx'), may hold values from -0.25 to 0.25
- w_down: bfloat16 [1536, 576], P('dp', 'ctx'), may hold values from -0.15625 to 0.15625
Outputs:
- output: bfloat16 [32, 2048, 576], P('dp', 'ctx')
- grad_tokens: float32 [32, 2048, 576], P('dp', 'ctx')
- grad_gain_attn: float32 [576], P('dp')
- grad_gain_mlp: float32 [576], P('dp')
- grad_query: float32 [576, 576], P('dp', 'ctx')
- grad_key: float32 [576, 192], P('dp', 'ctx')
- grad_value: float32 [576, 192], P('dp', 'ctx')
- grad_out: float32 [576, 576], P('dp', 'ctx')
- grad_gate: float32 [576, 1536], P('dp', 'ctx')
- grad_up: float32 [576, 1536], P('dp', 'ctx')
- grad_down: float32 [1536, 576], P('dp', 'ctx')
All inputs are finite; a program needn't handle non-finite values.
Results may differ from a plain program's by a relative error of at most 0.013.
Values may be sent and summed in bfloat16 or wider, within the bound.
A program may use at most 256 MiB of HBM per device.

v0:
```python
import jax
import jax.numpy as jnp
from jax import lax
from jax.sharding import PartitionSpec as P

HEADS = 9
KV_HEADS = 3
HEAD = 64


def positions_of(index, rows, ctx_size):
    half = rows // 2
    device = index // rows
    within = index % rows
    block = jnp.where(within < half, device, 2 * ctx_size - 1 - device)
    return block * half + within % half


def angles(pos, size):
    half = size // 2
    freq = 100000.0 ** (-jnp.arange(half, dtype=jnp.float32) * 2.0 / size)
    angle = pos.astype(jnp.float32)[:, None] * freq[None, :]
    return (jnp.cos(angle)[:, None, :], jnp.sin(angle)[:, None, :])


def rotate(vector, pos):
    half = vector.shape[-1] // 2
    cosine, sine = angles(pos, vector.shape[-1])
    first = vector[..., :half]
    second = vector[..., half:]
    return jnp.concatenate([first * cosine - second * sine, second * cosine + first * sine], -1)


def rotate_back(grad, pos):
    half = grad.shape[-1] // 2
    cosine, sine = angles(pos, grad.shape[-1])
    first = grad[..., :half]
    second = grad[..., half:]
    return jnp.concatenate([first * cosine + second * sine, second * cosine - first * sine], -1)


def matmul_left(left, right):
    return lax.dot_general(
        left, right, (((0,), (0,)), ((), ())), preferred_element_type=jnp.float32
    )


def matmul_right(left, right):
    return lax.dot_general(
        left, right, (((1,), (1,)), ((), ())), preferred_element_type=jnp.float32
    )


def shards(
    tokens, cotangent, gain_attn, gain_mlp, w_query, w_key, w_value, w_out, w_gate, w_up, w_down
):
    ctx_size = lax.axis_size("ctx")
    groups = HEADS // KV_HEADS
    kv_width = KV_HEADS * HEAD
    scale = HEAD ** (-0.5)
    columns = (
        lax.all_gather(w_query, "ctx", axis=1, tiled=True),
        lax.all_gather(w_key, "ctx", axis=1, tiled=True),
        lax.all_gather(w_value, "ctx", axis=1, tiled=True),
        lax.all_gather(w_out, "ctx", axis=1, tiled=True),
        lax.all_gather(w_gate, "ctx", axis=1, tiled=True),
        lax.all_gather(w_up, "ctx", axis=1, tiled=True),
        lax.all_gather(w_down, "ctx", axis=1, tiled=True),
    )
    full = (
        lax.all_gather(columns[0], "dp", axis=0, tiled=True),
        lax.all_gather(columns[1], "dp", axis=0, tiled=True),
        lax.all_gather(columns[2], "dp", axis=0, tiled=True),
        lax.all_gather(columns[3], "dp", axis=0, tiled=True),
        lax.all_gather(columns[4], "dp", axis=0, tiled=True),
        lax.all_gather(columns[5], "dp", axis=0, tiled=True),
        lax.all_gather(columns[6], "dp", axis=0, tiled=True),
        lax.all_gather(gain_attn, "dp", axis=0, tiled=True),
        lax.all_gather(gain_mlp, "dp", axis=0, tiled=True),
    )
    wq, wk, wv, wo, wg, wu, wd, gain_one, gain_two = full
    inputs = tokens[0].astype(jnp.float32)
    rows = inputs.shape[0]
    length = rows * ctx_size
    local_index = lax.axis_index("ctx") * rows + jnp.arange(rows, dtype=jnp.int32)
    pos_here = positions_of(local_index, rows, ctx_size)
    pos_all = positions_of(jnp.arange(length, dtype=jnp.int32), rows, ctx_size)
    allowed = pos_here[:, None] >= pos_all[None, :]
    gain_first = gain_one.astype(jnp.float32)
    gain_second = gain_two.astype(jnp.float32)
    scale_one = lax.rsqrt(jnp.mean(inputs * inputs, -1, keepdims=True) + 1e-05)
    normed = (inputs * scale_one * gain_first).astype(jnp.bfloat16)
    query_pre = jnp.dot(normed, wq, preferred_element_type=jnp.float32)
    key_pre = jnp.dot(normed, wk, preferred_element_type=jnp.float32)
    value_flat = jnp.dot(normed, wv, preferred_element_type=jnp.float32).astype(jnp.bfloat16)
    query = (
        rotate(query_pre.reshape(rows, HEADS, HEAD), pos_here)
        .astype(jnp.bfloat16)
        .reshape(rows, KV_HEADS, groups, HEAD)
    )
    key_flat = (
        rotate(key_pre.reshape(rows, KV_HEADS, HEAD), pos_here)
        .astype(jnp.bfloat16)
        .reshape(rows, kv_width)
    )
    key_gathered, value_gathered = (
        lax.all_gather(key_flat, "ctx", axis=0, tiled=True),
        lax.all_gather(value_flat, "ctx", axis=0, tiled=True),
    )
    key_all = key_gathered.reshape(length, KV_HEADS, HEAD)
    value_all = value_gathered.reshape(length, KV_HEADS, HEAD)

    def scores_of(keys):
        raw = jnp.einsum("qkgd,jkd->kgqj", query, keys, preferred_element_type=jnp.float32) * scale
        return jnp.where(allowed[None, None], raw, -1e30)

    scores = scores_of(key_all)
    top = jnp.max(scores, -1, keepdims=True)
    expd = jnp.exp(scores - top)
    denom = jnp.sum(expd, -1, keepdims=True)
    probs_low = (expd / denom).astype(jnp.bfloat16)
    log_total = top + jnp.log(denom)
    mixed = jnp.einsum("kgqj,jkd->qkgd", probs_low, value_all, preferred_element_type=jnp.float32)
    mixed = mixed.reshape(rows, HEADS * HEAD).astype(jnp.bfloat16)
    middle = inputs + jnp.dot(mixed, wo, preferred_element_type=jnp.float32)
    scale_two = lax.rsqrt(jnp.mean(middle * middle, -1, keepdims=True) + 1e-05)
    normed_two = (middle * scale_two * gain_second).astype(jnp.bfloat16)
    gate = jnp.dot(normed_two, wg, preferred_element_type=jnp.float32)
    upper = jnp.dot(normed_two, wu, preferred_element_type=jnp.float32)
    sigma = jax.nn.sigmoid(gate)
    silu_gate = gate * sigma
    hidden = (silu_gate * upper).astype(jnp.bfloat16)
    result = middle + jnp.dot(hidden, wd, preferred_element_type=jnp.float32)
    columns_back = (
        lax.all_gather(w_query, "ctx", axis=1, tiled=True),
        lax.all_gather(w_key, "ctx", axis=1, tiled=True),
        lax.all_gather(w_value, "ctx", axis=1, tiled=True),
        lax.all_gather(w_out, "ctx", axis=1, tiled=True),
        lax.all_gather(w_gate, "ctx", axis=1, tiled=True),
        lax.all_gather(w_up, "ctx", axis=1, tiled=True),
        lax.all_gather(w_down, "ctx", axis=1, tiled=True),
    )
    again = (
        lax.all_gather(columns_back[0], "dp", axis=0, tiled=True),
        lax.all_gather(columns_back[1], "dp", axis=0, tiled=True),
        lax.all_gather(columns_back[2], "dp", axis=0, tiled=True),
        lax.all_gather(columns_back[3], "dp", axis=0, tiled=True),
        lax.all_gather(columns_back[4], "dp", axis=0, tiled=True),
        lax.all_gather(columns_back[5], "dp", axis=0, tiled=True),
        lax.all_gather(columns_back[6], "dp", axis=0, tiled=True),
        lax.all_gather(gain_attn, "dp", axis=0, tiled=True),
        lax.all_gather(gain_mlp, "dp", axis=0, tiled=True),
    )
    wq_b, wk_b, wv_b, wo_b, wg_b, wu_b, wd_b = (
        again[0],
        again[1],
        again[2],
        again[3],
        again[4],
        again[5],
        again[6],
    )
    key_again, value_again = (
        lax.all_gather(key_flat, "ctx", axis=0, tiled=True),
        lax.all_gather(value_flat, "ctx", axis=0, tiled=True),
    )
    key_back = key_again.reshape(length, KV_HEADS, HEAD)
    value_back = value_again.reshape(length, KV_HEADS, HEAD)
    grad_result = cotangent[0]
    grad_float = grad_result.astype(jnp.float32)
    grad_down = matmul_left(hidden, grad_result)
    grad_hidden = matmul_right(grad_result, wd_b)
    grad_gate_in = (grad_hidden * upper * sigma * (1.0 + gate * (1.0 - sigma))).astype(jnp.bfloat16)
    grad_up_in = (grad_hidden * silu_gate).astype(jnp.bfloat16)
    grad_gate = matmul_left(normed_two, grad_gate_in)
    grad_upw = matmul_left(normed_two, grad_up_in)
    grad_normed_two = matmul_right(grad_gate_in, wg_b) + matmul_right(grad_up_in, wu_b)
    grad_gain_two = jnp.sum(grad_normed_two * middle * scale_two, 0)
    grad_middle = (
        grad_float
        + scale_two * gain_second * grad_normed_two
        - middle
        * scale_two**3
        * jnp.mean(middle * gain_second * grad_normed_two, -1, keepdims=True)
    )
    grad_attn = grad_middle.astype(jnp.bfloat16)
    grad_outw = matmul_left(mixed, grad_attn)
    grad_mixed = (
        matmul_right(grad_attn, wo_b).astype(jnp.bfloat16).reshape(rows, KV_HEADS, groups, HEAD)
    )
    probs = jnp.exp(scores_of(key_back) - log_total)
    probs_back = probs.astype(jnp.bfloat16)
    grad_probs = jnp.einsum(
        "qkgd,jkd->kgqj", grad_mixed, value_back, preferred_element_type=jnp.float32
    )
    weighted = jnp.sum(probs * grad_probs, -1, keepdims=True)
    grad_scores = (probs * (grad_probs - weighted)).astype(jnp.bfloat16)
    grad_query_rot = (
        jnp.einsum("kgqj,jkd->qkgd", grad_scores, key_back, preferred_element_type=jnp.float32)
        * scale
    )
    grad_keys = (
        jnp.einsum("kgqj,qkgd->jkd", grad_scores, query, preferred_element_type=jnp.float32) * scale
    )
    grad_values = jnp.einsum(
        "kgqj,qkgd->jkd", probs_back, grad_mixed, preferred_element_type=jnp.float32
    )
    kv_sums = lax.psum_scatter(
        jnp.stack(
            [
                grad_keys.reshape(lax.axis_size("ctx") * rows, kv_width),
                grad_values.reshape(lax.axis_size("ctx") * rows, kv_width),
            ],
            1,
        ),
        "ctx",
        scatter_dimension=0,
        tiled=True,
    )
    grad_key_pre = (
        rotate_back(kv_sums[:, 0].reshape(rows, KV_HEADS, HEAD), pos_here)
        .reshape(rows, kv_width)
        .astype(jnp.bfloat16)
    )
    grad_value_pre = kv_sums[:, 1].astype(jnp.bfloat16)
    grad_query_pre = (
        rotate_back(grad_query_rot.reshape(rows, HEADS, HEAD), pos_here)
        .reshape(rows, HEADS * HEAD)
        .astype(jnp.bfloat16)
    )
    grad_queryw = matmul_left(normed, grad_query_pre)
    grad_keyw = matmul_left(normed, grad_key_pre)
    grad_valuew = matmul_left(normed, grad_value_pre)
    grad_normed = (
        matmul_right(grad_query_pre, wq_b)
        + matmul_right(grad_key_pre, wk_b)
        + matmul_right(grad_value_pre, wv_b)
    )
    grad_gain_one = jnp.sum(grad_normed * inputs * scale_one, 0)
    grad_inputs = (
        grad_middle
        + scale_one * gain_first * grad_normed
        - inputs * scale_one**3 * jnp.mean(inputs * gain_first * grad_normed, -1, keepdims=True)
    )
    summed = (
        lax.psum_scatter(grad_queryw, "dp", scatter_dimension=0, tiled=True),
        lax.psum_scatter(grad_keyw, "dp", scatter_dimension=0, tiled=True),
        lax.psum_scatter(grad_valuew, "dp", scatter_dimension=0, tiled=True),
        lax.psum_scatter(grad_outw, "dp", scatter_dimension=0, tiled=True),
        lax.psum_scatter(grad_gate, "dp", scatter_dimension=0, tiled=True),
        lax.psum_scatter(grad_upw, "dp", scatter_dimension=0, tiled=True),
        lax.psum_scatter(grad_down, "dp", scatter_dimension=0, tiled=True),
        lax.psum_scatter(grad_gain_one, "dp", scatter_dimension=0, tiled=True),
        lax.psum_scatter(grad_gain_two, "dp", scatter_dimension=0, tiled=True),
    )
    tile_one = jnp.broadcast_to(summed[7][:, None], (summed[7].shape[0], ctx_size))
    tile_two = jnp.broadcast_to(summed[8][:, None], (summed[8].shape[0], ctx_size))
    final = (
        lax.psum_scatter(summed[0], "ctx", scatter_dimension=1, tiled=True),
        lax.psum_scatter(summed[1], "ctx", scatter_dimension=1, tiled=True),
        lax.psum_scatter(summed[2], "ctx", scatter_dimension=1, tiled=True),
        lax.psum_scatter(summed[3], "ctx", scatter_dimension=1, tiled=True),
        lax.psum_scatter(summed[4], "ctx", scatter_dimension=1, tiled=True),
        lax.psum_scatter(summed[5], "ctx", scatter_dimension=1, tiled=True),
        lax.psum_scatter(summed[6], "ctx", scatter_dimension=1, tiled=True),
        lax.psum_scatter(tile_one, "ctx", scatter_dimension=1, tiled=True),
        lax.psum_scatter(tile_two, "ctx", scatter_dimension=1, tiled=True),
    )
    return (
        result.astype(jnp.bfloat16)[None],
        grad_inputs[None],
        final[7].reshape(-1),
        final[8].reshape(-1),
        final[0],
        final[1],
        final[2],
        final[3],
        final[4],
        final[5],
        final[6],
    )


def solution(mesh):
    in_specs = (
        P("dp", "ctx", None),
        P("dp", "ctx", None),
        P("dp"),
        P("dp"),
        P("dp", "ctx"),
        P("dp", "ctx"),
        P("dp", "ctx"),
        P("dp", "ctx"),
        P("dp", "ctx"),
        P("dp", "ctx"),
        P("dp", "ctx"),
    )
    out_specs = (
        P("dp", "ctx", None),
        P("dp", "ctx", None),
        P("dp"),
        P("dp"),
        P("dp", "ctx"),
        P("dp", "ctx"),
        P("dp", "ctx"),
        P("dp", "ctx"),
        P("dp", "ctx"),
        P("dp", "ctx"),
        P("dp", "ctx"),
    )
    return jax.shard_map(shards, mesh=mesh, in_specs=in_specs, out_specs=out_specs, check_vma=False)
```

profile of v0, /device:TPU:0, one launch (start us, length us, event | category | flops | bytes accessed | tf_op | source)
XLA Modules:
  0.0 1478.0 jit_solution(10611093943562476438)
XLA Ops:
  7.3 9.4 all_gather.82
  16.7 7.5 all_gather.84
  24.4 7.1 all-gather.10
  32.4 7.0 all-gather
  39.5 83.2 %all-gather.1 = bf16[32,18,192]{2,1,0:T(8,128)(2,1)S(1)} all-gather(bf16[1,18,192]{2,1,0:T(8,128)(2,1)S(1)} %bitcast.259), channel_id=1, replica_groups=mesh['dp'=32,'ctx'=4] {'dp'}, dimensions={0}, use_global_device_ids=true | all-gather | bytes 228096 | tf_op jit(solution)/shard_map/all_gather | solution.py:73
  124.6 77.0 %all-reduce.19 = (bf16[576]{0:T(1024)(128)(2,1)S(1)}, bf16[576]{0:T(1024)(128)(2,1)S(1)}) all-reduce(bf16[576]{0:T(1024)(128)(2,1)S(1)} %dynamic-update-slice, bf16[576]{0:T(1024)(128)(2,1)S(1)} %dynamic-update-slice.1), channel_id=1, replica_groups=mesh['dp'=32,'ctx'=4] {'dp'}, use_global_device_ids=true, to_apply=%add | all-reduce | flops 1152 | bytes 4608
  202.8 11.0 all_gather.73
  220.7 79.4 %all-gather.3 = bf16[32,18,192]{2,1,0:T(8,128)(2,1)S(1)} all-gather(bf16[1,18,192]{2,1,0:T(8,128)(2,1)S(1)} %bitcast.260), channel_id=1, replica_groups=mesh['dp'=32,'ctx'=4] {'dp'}, dimensions={0}, use_global_device_ids=true | all-gather | bytes 228096 | tf_op jit(solution)/shard_map/all_gather | solution.py:72
  301.3 9.7 all_gather.76
  317.8 82.7 %all-gather.5 = bf16[32,18,576]{2,1,0:T(8,128)(2,1)S(1)} all-gather(bf16[1,18,576]{2,1,0:T(8,128)(2,1)S(1)} %bitcast.254), channel_id=1, replica_groups=mesh['dp'=32,'ctx'=4] {'dp'}, dimensions={0}, use_global_device_ids=true | all-gather | bytes 684288 | tf_op jit(solution)/shard_map/all_gather | solution.py:71
  403.2 15.2 %fusion.87 = (f32[3,3,512]{2,1,0:T(4,128)S(1)}, f32[3,3,512,2048]{2,3,1,0:T(8,128)}) fusion(bf16[2048,3,64,1]{0,2,3,1:T(8,128)(2,1)S(1)} %bitcast.232, bf16[512,3,3,32]{0,3,2,1:T(8,128)(2,1)S(1)} %bitcast.242, bf16[512,3,3,32]{0,3,2,1:T(8,128)(2,1)S(1)} %bitcast.240, pred[512,2048]{0,1:T(8,128)(4,1)S(1)} %broadcast_compare_fusion), kind=kOutput, calls=%fused_computation.150 | convolution fusion | flops 1237446144 | bytes 40192000 | tf_op jit(solution)/shard_map/qkgd,jkd->kgqj/dot_general | solution.py:114
  418.5 14.9 %fusion.7 = f32[3,3,512]{2,1,0:T(4,128)S(1)} fusion(f32[3,3,512,2048]{2,3,1,0:T(8,128)} %get-tuple-element.52, f32[3,3,512]{2,1,0:T(4,128)S(1)} %get-tuple-element.51), kind=kLoop, calls=%fused_computation.9 | loop fusion | flops 18869760 | bytes 37785600 | tf_op jit(solution)/shard_map/reduce_sum | solution.py:120
  433.4 14.7 fusion.22
  448.1 6.9 all-gather.6
  455.1 82.0 %all-gather.7 = bf16[32,18,576]{2,1,0:T(8,128)(2,1)S(1)} all-gather(bf16[1,18,576]{2,1,0:T(8,128)(2,1)S(1)} %bitcast.255), channel_id=1, replica_groups=mesh['dp'=32,'ctx'=4] {'dp'}, dimensions={0}, use_global_device_ids=true | all-gather | bytes 684288 | tf_op jit(solution)/shard_map/all_gather | solution.py:74
  570.3 28.9 %fusion.4 = (f32[3,3,512]{2,1,0:T(4,128)}, f32[3,2048,512,3]{2,1,3,0:T(8,128)}) fusion(f32[3,3,512,2048]{2,3,1,0:T(8,128)} %get-tuple-element.52, f32[3,3,512]{2,1,0:T(4,128)} %log_add_fusion, bf16[2048,3,64,1]{0,2,3,1:T(8,128)(2,1)} %bitcast.230, bf16[512,3,3,64]{0,3,2,1:T(8,128)(2,1)} %bitcast.226), kind=kOutput, calls=%fused_computation.2 | convolution fusion | flops 1236266496 | bytes 76910592 | tf_op jit(solution)/shard_map/qkgd,jkd->kgqj/dot_general | solution.py:193
  599.3 31.3 %fusion.6 = bf16[3,3,512,2048]{2,3,1,0:T(8,128)(2,1)} fusion(f32[3,2048,512,3]{2,1,3,0:T(8,128)} %get-tuple-element.57, f32[3,3,512,2048]{2,3,1,0:T(8,128)} %get-tuple-element.52, f32[3,3,512]{2,1,0:T(4,128)} %get-tuple-element.56, f32[3,3,512]{2,1,0:T(4,128)} %log_add_fusion), kind=kLoop, calls=%fused_computation.4 | loop fusion | flops 37748736 | bytes 94408704 | tf_op jit(solution)/shard_map/convert_element_type | solution.py:197
  630.6 8.7 convolution_multiply_fusion
  642.3 13.6 fusion.14
  655.9 16.3 %fusion.9 = f32[3,64,2048,1]{2,1,3,0:T(8,128)} fusion(bf16[512,3,3,64]{0,3,2,1:T(8,128)(2,1)} %bitcast.227, f32[3,3,512,2048]{2,3,1,0:T(8,128)} %get-tuple-element.52, f32[3,3,512]{2,1,0:T(4,128)} %log_add_fusion), kind=kOutput, calls=%fused_computation.11 | convolution fusion | flops 1226833920 | bytes 39929856 | tf_op jit(solution)/shard_map/kgqj,qkgd->jkd/dot_general | solution.py:205
  676.9 274.7 %all-reduce.23.cloned.1.call-done = (f32[576,576]{1,0:T(8,128)}, f32[576,576]{1,0:T(8,128)}) async-done(((f32[576,576]{1,0:T(8,128)}, f32[576,576]{1,0:T(8,128)}), (f32[576,576]{1,0:T(8,128)}, f32[576,576]{1,0:T(8,128)})) %all-reduce.23.cloned.1.call-update) | async-done | bytes 2654224
  970.8 26.1 %reduce-scatter.28.cloned.1.call-done = f32[512,2,192]{0,2,1:T(8,128)} async-done(((f32[2048,2,192]{0,2,1:T(8,128)}), f32[512,2,192]{0,2,1:T(8,128)}) %reduce-scatter.28.cloned.1.call-update) | async-done | bytes 786448 | tf_op jit(solution)/shard_map/reduce_scatter | solution.py:208
  1001.2 130.3 %fusion.85 = (f32[24,192]{1,0:T(8,128)}, f32[24,192]{1,0:T(8,128)}, f32[24,1536]{1,0:T(8,128)}, f32[24,1536]{1,0:T(8,128)}) fusion(f32[576,192]{1,0:T(8,128)} %fusion.49, f32[576,192]{1,0:T(8,128)S(1)} %fusion.47, f32[576,1536]{1,0:T(8,128)} %fusion.91, f32[576,1536]{1,0:T(8,128)} %fusion.92), kind=kCustom, calls=%all-reduce-scatter.4 | all-reduce-scatter fusion | flops 2654209 | bytes 8294912
  1200.3 12.5 concatenate.26
  1214.7 11.8 concatenate.25
  1242.0 80.2 %all-reduce.16 = (f32[576]{0:T(1024)}, f32[576]{0:T(1024)}) all-reduce(f32[576]{0:T(1024)S(1)} %get-tuple-element.13, f32[576]{0:T(1024)} %get-tuple-element.11), channel_id=3, replica_groups=mesh['dp'=32,'ctx'=4] {'dp'}, use_global_device_ids=true, to_apply=%region_9.10.clone | all-reduce | flops 1152 | bytes 9216
  1324.3 8.1 all-reduce.18
  1342.3 14.7 concatenate.27
  1369.2 14.3 concatenate.28
  1389.3 24.1 %reduce-scatter.44.cloned.1.call-done = f32[144,48]{1,0:T(8,128)} async-done(((f32[576,48]{1,0:T(8,128)}), f32[144,48]{1,0:T(8,128)}) %reduce-scatter.44.cloned.1.call-update) | async-done | bytes 27664
  1415.0 27.3 %reduce-scatter.30.cloned.1.call-done = f32[18,384]{1,0:T(8,128)} async-done(((f32[18,1536]{1,0:T(8,128)}), f32[18,384]{1,0:T(8,128)}) %reduce-scatter.30.cloned.1.call-update) | async-done | bytes 27664 | tf_op jit(solution)/shard_map/reduce_scatter | solution.py:263
  1442.3 29.0 %reduce-scatter.32.cloned.1.call-done = f32[18,384]{1,0:T(8,128)} async-done(((f32[18,1536]{1,0:T(8,128)}), f32[18,384]{1,0:T(8,128)}) %reduce-scatter.32.cloned.1.call-update) | async-done | bytes 27664 | tf_op jit(solution)/shard_map/reduce_scatter | solution.py:264
  (304 shorter events, 201.4 us)
Async XLA Ops:
  7.2 532.4 %all-gather.17.cloned.1.call-start = ((), (), s32[]{:S(2)}) async-start(), calls=%async_computation.14 | async-start | bytes 2433024 | tf_op jit(solution)/shard_map/all_gather | solution.py:75
  16.7 527.0 %all-gather.19.cloned.1.call-start = ((), (), s32[]{:S(2)}) async-start(), calls=%async_computation.15 | async-start | bytes 2433024 | tf_op jit(solution)/shard_map/all_gather | solution.py:76
  24.3 531.0 %all-gather.15.cloned.1.call-start = ((), (), s32[]{:S(2)}) async-start(), calls=%async_computation.9 | async-start | bytes 2027520 | tf_op jit(solution)/shard_map/all_gather | solution.py:77
  32.3 919.3 %all-reduce.23.cloned.1.call-start = ((), (), s32[]{:S(2)}) async-start(), calls=%async_computation.21 | async-start | bytes 5898240
  642.2 354.7 %reduce-scatter.28.cloned.1.call-start = ((), (), s32[]{:S(2)}) async-start(), calls=%async_computation.10 | async-start | bytes 3932160 | tf_op jit(solution)/shard_map/reduce_scatter | solution.py:208
  676.2 492.1 %reduce-scatter.36.cloned.1.call-start = ((), (), s32[]{:S(2)}) async-start(), calls=%async_computation.16 | async-start | bytes 368640
  954.8 215.1 %reduce-scatter.42.cloned.1.call-start = ((), (), s32[]{:S(2)}) async-start(), calls=%async_computation.19 | async-start | bytes 368640
  956.6 400.4 %reduce-scatter.34.cloned.1.call-start = ((), (), s32[]{:S(2)}) async-start(), calls=%async_computation.13 | async-start | bytes 4055040 | tf_op jit(solution)/shard_map/reduce_scatter | solution.py:252
  961.6 424.9 %reduce-scatter.38.cloned.1.call-start = ((), (), s32[]{:S(2)}) async-start(), calls=%async_computation.17 | async-start | bytes 122880
  1132.3 24.4 %collective-permute-start.14 = (f32[24,192]{1,0:T(8,128)}, f32[24,192]{1,0:T(8,128)S(1)}, u32[]{:S(2)}, u32[]{:S(2)}) collective-permute-start(f32[24,192]{1,0:T(8,128)} %get-tuple-element.28), channel_id=1, source_target_pairs={{0,28},{4,32},{8,36},{12,40},{16,44},{20,48},{24,52},{28,56},{32,6... | collective-permute-start | bytes 55304
  1133.5 27.2 %collective-permute-start.13 = (f32[24,192]{1,0:T(8,128)}, f32[24,192]{1,0:T(8,128)S(1)}, u32[]{:S(2)}, u32[]{:S(2)}) collective-permute-start(f32[24,192]{1,0:T(8,128)} %get-tuple-element.28), channel_id=1, source_target_pairs={{0,24},{4,28},{8,32},{12,36},{16,40},{20,44},{24,48},{28,52},{32,5... | collective-permute-start | bytes 55304
  1135.2 28.0 %collective-permute-start.12 = (f32[24,192]{1,0:T(8,128)}, f32[24,192]{1,0:T(8,128)S(1)}, u32[]{:S(2)}, u32[]{:S(2)}) collective-permute-start(f32[24,192]{1,0:T(8,128)} %get-tuple-element.28), channel_id=1, source_target_pairs={{0,20},{4,24},{8,28},{12,32},{16,36},{20,40},{24,44},{28,48},{32,5... | collective-permute-start | bytes 55304
  1149.4 22.1 %collective-permute-start.11 = (f32[24,192]{1,0:T(8,128)S(1)}, f32[24,192]{1,0:T(8,128)}, u32[]{:S(2)}, u32[]{:S(2)}) collective-permute-start(f32[24,192]{1,0:T(8,128)S(1)} %copy-done.35), channel_id=1, source_target_pairs={{0,16},{4,20},{8,24},{12,28},{16,32},{20,36},{24,40},{28,44},{32,4... | collective-permute-start | bytes 55304
  1152.5 20.5 %collective-permute-start.10 = (f32[24,192]{1,0:T(8,128)S(1)}, f32[24,192]{1,0:T(8,128)}, u32[]{:S(2)}, u32[]{:S(2)}) collective-permute-start(f32[24,192]{1,0:T(8,128)S(1)} %copy-done.35), channel_id=1, source_target_pairs={{0,12},{4,16},{8,20},{12,24},{16,28},{20,32},{24,36},{28,40},{32,4... | collective-permute-start | bytes 55304
  1156.7 17.7 %collective-permute-start.9 = (f32[24,192]{1,0:T(8,128)S(1)}, f32[24,192]{1,0:T(8,128)}, u32[]{:S(2)}, u32[]{:S(2)}) collective-permute-start(f32[24,192]{1,0:T(8,128)S(1)} %copy-done.35), channel_id=1, source_target_pairs={{0,8},{4,12},{8,16},{12,20},{16,24},{20,28},{24,32},{28,36},{32,40... | collective-permute-start | bytes 55304
  1183.5 29.3 %collective-permute-start = (f32[24,192]{1,0:T(8,128)S(1)}, f32[24,192]{1,0:T(8,128)}, u32[]{:S(2)}, u32[]{:S(2)}) collective-permute-start(f32[24,192]{1,0:T(8,128)S(1)} %copy-done.34), channel_id=1, source_target_pairs={{0,4},{4,8},{8,12},{12,16},{16,20},{20,24},{24,28},{28,32},{32,36}... | collective-permute-start | bytes 55304
  1186.0 46.0 %collective-permute-start.22 = (f32[24,1536]{1,0:T(8,128)S(1)}, f32[24,1536]{1,0:T(8,128)}, u32[]{:S(2)}, u32[]{:S(2)}) collective-permute-start(f32[24,1536]{1,0:T(8,128)S(1)} %copy-done.28), channel_id=1, source_target_pairs={{0,28},{4,32},{8,36},{12,40},{16,44},{20,48},{24,52},{28,56},{32,6... | collective-permute-start | bytes 442376
  1190.0 44.7 %collective-permute-start.21 = (f32[24,1536]{1,0:T(8,128)S(1)}, f32[24,1536]{1,0:T(8,128)}, u32[]{:S(2)}, u32[]{:S(2)}) collective-permute-start(f32[24,1536]{1,0:T(8,128)S(1)} %copy-done.28), channel_id=1, source_target_pairs={{0,24},{4,28},{8,32},{12,36},{16,40},{20,44},{24,48},{28,52},{32,5... | collective-permute-start | bytes 442376
  1193.5 43.8 %collective-permute-start.20 = (f32[24,1536]{1,0:T(8,128)S(1)}, f32[24,1536]{1,0:T(8,128)}, u32[]{:S(2)}, u32[]{:S(2)}) collective-permute-start(f32[24,1536]{1,0:T(8,128)S(1)} %copy-done.28), channel_id=1, source_target_pairs={{0,20},{4,24},{8,28},{12,32},{16,36},{20,40},{24,44},{28,48},{32,5... | collective-permute-start | bytes 442376
  1196.3 43.1 %collective-permute-start.19 = (f32[24,1536]{1,0:T(8,128)S(1)}, f32[24,1536]{1,0:T(8,128)}, u32[]{:S(2)}, u32[]{:S(2)}) collective-permute-start(f32[24,1536]{1,0:T(8,128)S(1)} %copy-done.28), channel_id=1, source_target_pairs={{0,16},{4,20},{8,24},{12,28},{16,32},{20,36},{24,40},{28,44},{32,4... | collective-permute-start | bytes 442376
  1228.7 159.2 %reduce-scatter.40.cloned.1.call-start = ((), (), s32[]{:S(2)}) async-start(), calls=%async_computation.18 | async-start | bytes 122880
  1228.7 105.2 %collective-permute-start.18 = (f32[24,1536]{1,0:T(8,128)S(1)}, f32[24,1536]{1,0:T(8,128)}, u32[]{:S(2)}, u32[]{:S(2)}) collective-permute-start(f32[24,1536]{1,0:T(8,128)S(1)} %copy-done.28), channel_id=1, source_target_pairs={{0,12},{4,16},{8,20},{12,24},{16,28},{20,32},{24,36},{28,40},{32,4... | collective-permute-start | bytes 442376
  1231.9 105.8 %collective-permute-start.17 = (f32[24,1536]{1,0:T(8,128)S(1)}, f32[24,1536]{1,0:T(8,128)}, u32[]{:S(2)}, u32[]{:S(2)}) collective-permute-start(f32[24,1536]{1,0:T(8,128)S(1)} %copy-done.28), channel_id=1, source_target_pairs={{0,8},{4,12},{8,16},{12,20},{16,24},{20,28},{24,32},{28,36},{32,40... | collective-permute-start | bytes 442376
  1234.7 104.9 %collective-permute-start.16 = (f32[24,1536]{1,0:T(8,128)S(1)}, f32[24,1536]{1,0:T(8,128)}, u32[]{:S(2)}, u32[]{:S(2)}) collective-permute-start(f32[24,1536]{1,0:T(8,128)S(1)} %copy-done.28), channel_id=1, source_target_pairs={{0,4},{4,8},{8,12},{12,16},{16,20},{20,24},{24,28},{28,32},{32,36}... | collective-permute-start | bytes 442376
  1237.3 122.9 %collective-permute-start.30 = (f32[24,1536]{1,0:T(8,128)S(1)}, f32[24,1536]{1,0:T(8,128)S(1)}, u32[]{:S(2)}, u32[]{:S(2)}) collective-permute-start(f32[24,1536]{1,0:T(8,128)S(1)} %copy-done.27), channel_id=1, source_target_pairs={{0,28},{4,32},{8,36},{12,40},{16,44},{20,48},{24,52},{28,56},{32,6... | collective-permute-start | bytes 442376
  1239.4 124.1 %collective-permute-start.29 = (f32[24,1536]{1,0:T(8,128)S(1)}, f32[24,1536]{1,0:T(8,128)}, u32[]{:S(2)}, u32[]{:S(2)}) collective-permute-start(f32[24,1536]{1,0:T(8,128)S(1)} %copy-done.27), channel_id=1, source_target_pairs={{0,24},{4,28},{8,32},{12,36},{16,40},{20,44},{24,48},{28,52},{32,5... | collective-permute-start | bytes 442376
  1333.9 79.5 %reduce-scatter.44.cloned.1.call-start = ((), (), s32[]{:S(2)}) async-start(), calls=%async_computation.20 | async-start | bytes 368640
  1334.0 24.9 %collective-permute-start.31 = (f32[18,1536]{1,0:T(8,128)S(1)}, f32[18,1536]{1,0:T(8,128)}, u32[]{:S(2)}, u32[]{:S(2)}) collective-permute-start(f32[18,1536]{1,0:T(8,128)S(1)} %slice.53), channel_id=1, source_target_pairs={{0,32},{4,36},{8,40},{12,44},{16,48},{20,52},{24,56},{28,60},{32,6... | collective-permute-start | bytes 331784
  1337.7 29.5 %collective-permute-start.28 = (f32[24,1536]{1,0:T(8,128)S(1)}, f32[24,1536]{1,0:T(8,128)}, u32[]{:S(2)}, u32[]{:S(2)}) collective-permute-start(f32[24,1536]{1,0:T(8,128)S(1)} %copy-done.27), channel_id=1, source_target_pairs={{0,20},{4,24},{8,28},{12,32},{16,36},{20,40},{24,44},{28,48},{32,5... | collective-permute-start | bytes 442376
  1339.6 27.6 %collective-permute-start.27 = (f32[24,1536]{1,0:T(8,128)S(1)}, f32[24,1536]{1,0:T(8,128)}, u32[]{:S(2)}, u32[]{:S(2)}) collective-permute-start(f32[24,1536]{1,0:T(8,128)S(1)} %copy-done.27), channel_id=1, source_target_pairs={{0,16},{4,20},{8,24},{12,28},{16,32},{20,36},{24,40},{28,44},{32,4... | collective-permute-start | bytes 442376
  1358.8 83.5 %reduce-scatter.30.cloned.1.call-start = ((), (), s32[]{:S(2)}) async-start(), calls=%async_computation.11 | async-start | bytes 184320 | tf_op jit(solution)/shard_map/reduce_scatter | solution.py:263
  1367.1 104.2 %reduce-scatter.32.cloned.1.call-start = ((), (), s32[]{:S(2)}) async-start(), calls=%async_computation.12 | async-start | bytes 184320 | tf_op jit(solution)/shard_map/reduce_scatter | solution.py:264
  (68 other events, 1774.5 us)
Sparse Core Ops, SparseCore 0:
  16.8 154.8 all-gather.16
  173.4 154.3 all-gather.18
  329.5 154.1 all-gather.14
  642.4 309.1 all-reduce.22
  954.2 42.6 reduce-scatter.27
  999.3 129.7 reduce-scatter.35
  1131.9 26.4 reduce-scatter.41
  1160.8 168.7 reduce-scatter.33
  1332.3 23.3 reduce-scatter.37
  1358.2 25.7 reduce-scatter.39
  1386.8 26.5 reduce-scatter.43
  1416.4 25.8 reduce-scatter.29
  1445.4 25.8 reduce-scatter.31
where the time goes:
time: 1490 us; the launch traced here: 1480 us
  blocking collectives  695 us (47%)
  waiting for transfers between devices  384 us (26%)
  matrix products  142 us (10%)
  local copies, waits for them, and re-layouts  98.7 us (7%)
  starting transfers between devices  84.4 us (6%)
  other arithmetic  57.2 us (4%)
  between operations  17 us (1%)
    unnamed x51, waiting for transfers between devices  301 us
    unnamed x4, blocking collectives  296 us
    unnamed x151, local copies, waits for them, and re-layouts  94.6 us
    unnamed x38, starting transfers between devices  84.1 us
    all_gather x1, blocking collectives, shards(): lax.all_gather(columns[2], 'dp', axis=0, tiled=True)  83.2 us
    all_gather x1, blocking collectives, shards(): lax.all_gather(columns[0], 'dp', axis=0, tiled=True)  82.7 us
    all_gather x1, blocking collectives, shards(): lax.all_gather(columns[3], 'dp', axis=0, tiled=True)  82 us
    all_gather x1, blocking collectives, shards(): lax.all_gather(columns[1], 'dp', axis=0, tiled=True)  79.4 us
  transfers between devices with their start and end apart: 45, of which 7 were waited for; matrix products, arithmetic and copies ran while one was open for 23% of the time, Pallas kernels for 0%

commit v1 on v0

v1 whole, which is shorter than its diff:
```python
import functools

import jax
import jax.numpy as jnp
import numpy as np
from jax import lax
from jax.experimental import pallas as pl
from jax.experimental.pallas import tpu as pltpu
from jax.sharding import PartitionSpec as P

D = 576
HEADS = 9
KV_HEADS = 3
HEAD = 64
GROUP = HEADS // KV_HEADS
FF = 1536
KV = KV_HEADS * HEAD
MESH = pl.DeviceIdType.MESH
BF = jnp.bfloat16
F32 = jnp.float32

EARLY = 48
LATE = 192
EARLY_STREAMS = ((0, 16, (0, 1, 2)), (16, 32, (1, 2, 0)), (32, 48, (2, 0, 1)))
LATE_GATHER = ((0, 80, (2, 1, 0)), (80, 160, (2, 0, 1)), (160, 192, (0, 1, 2)))
LATE_REDUCE = ((0, 80, (0, 1, 2)), (80, 160, (1, 0, 2)), (160, 192, (2, 0, 1)))
UP_AT, DOWN_AT, TAIL_AT, OUT_AT = 54, 112, 160, 168
VMEM_LIMIT = 60 * 1024 * 1024


class Place:
    def __init__(self, sides):
        self.sides = sides
        nx, ny, nz = sides
        self.low = nz // 2
        dp = lax.axis_index("dp")
        ctx = lax.axis_index("ctx")
        x = dp // (self.low * ny)
        y = dp % ny
        z = (ctx // 2) * self.low + (dp // ny) % self.low
        self.at = (x, y, z)
        self.core = ctx % 2

    def device(self, at, core):
        x, y, z = at
        dp = (x * self.low + z % self.low) * self.sides[1] + y
        return (dp, (z // self.low) * 2 + core)

    def shifted(self, axis, step):
        at = list(self.at)
        n = self.sides[axis]
        at[axis] = lax.rem(at[axis] + (step + n), n)
        return tuple(at)

    def peer(self, axis, step):
        return self.device(self.shifted(axis, step), self.core)

    def sibling(self):
        return self.device(self.at, 1 - self.core)


def greet(place):
    barrier = pltpu.get_barrier_semaphore()
    friends = [place.sibling()]
    for axis in range(3):
        for step in range(1, place.sides[axis]):
            friends.append(place.peer(axis, step))
    for friend in friends:
        pl.semaphore_signal(barrier, inc=1, device_id=friend, device_id_type=MESH)
    pl.semaphore_wait(barrier, len(friends))


def remote(src, dst, send_sem, recv_sem, device):
    return pltpu.make_async_remote_copy(
        src_ref=src,
        dst_ref=dst,
        send_sem=send_sem,
        recv_sem=recv_sem,
        device_id=device,
        device_id_type=MESH,
    )


class Gather:
    def __init__(self, place, streams, slot_ref, out_ref, sems):
        self.place, self.streams = place, streams
        self.slot_ref, self.out_ref = slot_ref, out_ref
        self.local_sem, self.send_sem, self.recv_sem, self.pair_send, self.pair_recv = sems
        self.sends = [[] for _ in streams]
        self.pairs = []

    def region(self, free, at, lo, hi):
        index = tuple(slice(None) if axis in free else at[axis] for axis in range(3))
        return self.out_ref.at[(self.place.core,) + index + (pl.ds(lo, hi - lo),)]

    def exchange(self, number, phase, src, free, axis, lo, hi):
        for step in range(1, self.place.sides[axis]):
            copy = remote(
                src,
                self.region(free, self.place.at, lo, hi),
                self.send_sem.at[number, phase, step - 1],
                self.recv_sem.at[number, phase, step - 1],
                self.place.peer(axis, step),
            )
            copy.start()
            self.sends[number].append(copy)

    def start(self):
        for number, (lo, hi, order) in enumerate(self.streams):
            src = self.slot_ref.at[pl.ds(lo, hi - lo)]
            self.exchange(number, 0, src, (), order[0], lo, hi)
        own = self.out_ref.at[(self.place.core,) + self.place.at]
        self.local = pltpu.make_async_copy(self.slot_ref, own, self.local_sem)
        self.local.start()

    def relay(self, number, step, at, lo, hi, order):
        plane = self.region(order[:2], at, lo, hi)
        copy = remote(
            plane,
            plane,
            self.pair_send.at[number, step],
            self.pair_recv.at[number, step],
            self.place.sibling(),
        )
        copy.start()
        self.pairs.append(copy)

    def phase(self, phase):
        if phase == 1:
            self.local.wait()
        for number, (lo, hi, order) in enumerate(self.streams):
            for copy in self.sends[number][-(self.place.sides[order[phase - 1]] - 1) :]:
                copy.wait_recv()
            free = order[:phase]
            src = self.region(free, self.place.at, lo, hi)
            self.exchange(number, phase, src, free, order[phase], lo, hi)
        if phase == 2:
            for number, (lo, hi, order) in enumerate(self.streams):
                self.relay(number, 0, self.place.at, lo, hi, order)

    def arrive(self, step):
        for number, (lo, hi, order) in enumerate(self.streams):
            axis = order[2]
            if step < self.place.sides[axis]:
                self.sends[number][step - self.place.sides[axis]].wait_recv()
                self.relay(number, step, self.place.shifted(axis, -step), lo, hi, order)

    def finish(self):
        for group in self.sends:
            for copy in group:
                copy.wait_send()
        for copy in self.pairs:
            copy.wait()


def gather_sems(sides, streams):
    n, side = len(streams), max(sides)
    return [
        pltpu.SemaphoreType.DMA,
        pltpu.SemaphoreType.DMA((n, 3, side - 1)),
        pltpu.SemaphoreType.DMA((n, 3, side - 1)),
        pltpu.SemaphoreType.DMA((n, side)),
        pltpu.SemaphoreType.DMA((n, side)),
    ]


class Reduce:
    def __init__(self, place, streams, grads_ref, out_ref, scratch):
        self.place, self.streams = place, streams
        self.grads_ref, self.out_ref = grads_ref, out_ref
        self.pair, self.first, self.second, self.third = scratch[:4]
        self.pair_send, self.pair_recv, self.send_sem, self.recv_sem = scratch[4:]
        self.side = place.sides[0]
        self.sends = [[] for _ in streams]

    def start(self):
        self.swaps = []
        core = self.place.core
        for number, (lo, hi, order) in enumerate(self.streams):
            rows = pl.ds(lo, hi - lo)
            copy = remote(
                self.grads_ref.at[1 - core, :, :, :, rows],
                self.pair.at[:, :, :, rows],
                self.pair_send.at[number],
                self.pair_recv.at[number],
                self.place.sibling(),
            )
            copy.start()
            self.swaps.append(copy)

    def place_of(self, order, coords):
        index = [None, None, None]
        for axis, coord in zip(order, coords):
            index[axis] = coord
        return tuple(index)

    def exchange(self, number, phase, buffers, order, lo, hi):
        rows = pl.ds(lo, hi - lo)
        place, axis = self.place, order[phase]
        for step in range(1, self.side):
            fixed = [place.at[order[i]] for i in range(phase)]
            coords = fixed + [place.shifted(axis, step)[axis]] + [slice(None)] * (2 - phase)
            copy = remote(
                self.grads_ref.at[(place.core,) + self.place_of(order, coords) + (rows,)],
                buffers.at[(step - 1,) + (slice(None),) * (2 - phase) + (rows,)],
                self.send_sem.at[number, phase, step - 1],
                self.recv_sem.at[number, phase, step - 1],
                place.peer(axis, step),
            )
            copy.start()
            self.sends[number].append(copy)

    def arrived(self, number, phase):
        for copy in self.sends[number][phase * (self.side - 1) : (phase + 1) * (self.side - 1)]:
            copy.wait_recv()

    def phase_pair(self):
        held, pair, side, core = self.grads_ref, self.pair, self.side, self.place.core
        for number, (lo, hi, order) in enumerate(self.streams):
            rows = pl.ds(lo, hi - lo)
            self.swaps[number].wait_recv()

            def add(i, carry, rows=rows):
                a, b = i // side, i % side
                for c in range(side):
                    at = (core, a, b, c, rows)
                    held[at] = (held[at].astype(F32) + pair[at[1:]].astype(F32)).astype(BF)
                return carry

            lax.fori_loop(0, side * side, add, 0)
            self.exchange(number, 0, self.first, order, lo, hi)

    def phase_first(self):
        held, first, side, place = self.grads_ref, self.first, self.side, self.place
        for number, (lo, hi, order) in enumerate(self.streams):
            rows = pl.ds(lo, hi - lo)
            self.arrived(number, 0)

            def add(i, carry, rows=rows, order=order):
                b, c = i // side, i % side
                axes = (order[0],) + tuple(sorted(order[1:]))
                at = self.place_of(axes, (place.at[order[0]], b, c)) + (rows,)
                at = (place.core,) + at
                total = held[at].astype(F32)
                for step in range(side - 1):
                    total += first[step, b, c, rows].astype(F32)
                held[at] = total.astype(BF)
                return carry

            lax.fori_loop(0, side * side, add, 0)
            self.exchange(number, 1, self.second, order, lo, hi)

    def phase_second(self):
        held, second, side, place = self.grads_ref, self.second, self.side, self.place
        for number, (lo, hi, order) in enumerate(self.streams):
            rows = pl.ds(lo, hi - lo)
            self.arrived(number, 1)

            def add(c, carry, rows=rows, order=order):
                at = self.place_of(order, (place.at[order[0]], place.at[order[1]], c)) + (rows,)
                at = (place.core,) + at
                total = held[at].astype(F32)
                for step in range(side - 1):
                    total += second[step, c, rows].astype(F32)
                held[at] = total.astype(BF)
                return carry

            lax.fori_loop(0, side, add, 0)
            self.exchange(number, 2, self.third, order, lo, hi)

    def finish(self):
        for number, (lo, hi, order) in enumerate(self.streams):
            rows = pl.ds(lo, hi - lo)
            self.arrived(number, 2)
            total = self.grads_ref[(self.place.core,) + self.place.at + (rows,)].astype(F32)
            for step in range(self.side - 1):
                total += self.third[step, rows].astype(F32)
            self.out_ref[rows] = total
        for copy in self.swaps:
            copy.wait_send()
        for group in self.sends:
            for copy in group:
                copy.wait_send()


def reduce_scratch(sides, rows, streams):
    n, side = len(streams), sides[0]
    return [
        pltpu.VMEM(sides + (rows, 128), BF),
        pltpu.VMEM((side - 1, side, side, rows, 128), BF),
        pltpu.VMEM((side - 1, side, rows, 128), BF),
        pltpu.VMEM((side - 1, rows, 128), BF),
        pltpu.SemaphoreType.DMA((n,)),
        pltpu.SemaphoreType.DMA((n,)),
        pltpu.SemaphoreType.DMA((n, 3, side - 1)),
        pltpu.SemaphoreType.DMA((n, 3, side - 1)),
    ]


def pack_rows(pieces, rows):
    have = sum(piece.shape[0] for piece in pieces)
    if have < rows:
        pieces = pieces + [jnp.zeros((rows - have, 128), pieces[0].dtype)]
    return jnp.concatenate(pieces, 0)


def thin(block, count):
    return [block[:, 128 * t : 128 * t + 128] for t in range(count)]


def down_tail(tail):
    pieces = [tail[8 * b : 8 * b + 8] for b in range(6)]
    return jnp.concatenate(pieces + [jnp.zeros((8, 32), tail.dtype)], 1)


def open_tail(part):
    return jnp.concatenate([part[:, 16 * b : 16 * b + 16] for b in range(6)], 0)


def pack_weights(wq, wk, wv, wo, wg, wu, wd, gains, early_ref, late_ref):
    f = lambda ref: ref[...].astype(F32)
    out = f(wo)
    small = jnp.concatenate([f(wq), f(wk), f(wv), out[:, 128:]], 1)
    gain = jnp.concatenate([f(ref) for ref in gains], 0)
    gain = jnp.concatenate([gain, jnp.zeros((2, 128 - gain.shape[1]), F32)], 1)
    early_ref[...] = pack_rows(thin(small, 2) + [gain], EARLY).astype(BF)
    down = f(wd)
    late_ref[0:DOWN_AT] = pack_rows(thin(f(wg), 3) + thin(f(wu), 3), DOWN_AT).astype(BF)
    late_ref[DOWN_AT:TAIL_AT] = down[:, :128].astype(BF)
    tail = pack_rows([down_tail(down[:, 128:]), out[:, :128]], LATE - TAIL_AT)
    late_ref[TAIL_AT:LATE] = tail.astype(BF)


def unpack_early(slots, wqkv, tails):
    def block(x, carry):
        smalls = []
        for ctx in range(4):
            zh, core = ctx // 2, ctx % 2
            small = []
            for i in range(8):
                small.append(slots[core, x, i % 4, zh * 2 + i // 4].astype(F32))
            stack = lambda t: jnp.concatenate([b[18 * t : 18 * t + 18] for b in small], 0)
            smalls.append(jnp.concatenate([stack(t) for t in range(2)], 1))
        cut = lambda lo, hi: [part[:, lo:hi] for part in smalls]
        rows = pl.ds(pl.multiple_of(144 * x, 16), 144)
        whole = jnp.concatenate(cut(0, 144) + cut(144, 192) + cut(192, 240), 1)
        wqkv[rows, :] = whole.astype(BF)
        tails[rows, :] = jnp.concatenate(cut(240, 256), 1)
        return carry

    lax.fori_loop(0, 4, block, 0)


def unpack_gains(slots):
    pieces = []
    for x in range(4):
        for i in range(8):
            tile = slots[0, x, i % 4, i // 4, 32:48, :].astype(F32)
            pieces.append(tile[4:6, :18])
    return jnp.concatenate(pieces, 1)


def unpack_late(slots, tails, wo, wg, wu, wd):
    def block(x, carry):
        downs, outs = [[] for _ in range(8)], []
        rows = pl.ds(pl.multiple_of(144 * x, 16), 144)
        for ctx in range(4):
            zh, core = ctx // 2, ctx % 2
            gate, up, out = [], [], []
            for i in range(8):
                at = (core, x, i % 4, zh * 2 + i // 4)
                slot = slots[at].astype(F32)
                gate.append(slot[:UP_AT])
                up.append(slot[UP_AT : 2 * UP_AT])
                out.append(slot[OUT_AT : OUT_AT + 18])
                downs[i] += [slot[DOWN_AT:TAIL_AT], open_tail(slot[TAIL_AT:OUT_AT])]
            for t in range(3):
                lanes = slice(ctx * 384 + 128 * t, ctx * 384 + 128 * t + 128)
                stack = lambda blocks: jnp.concatenate(
                    [b[18 * t : 18 * t + 18] for b in blocks], 0
                )
                wg[rows, lanes] = stack(gate).astype(BF)
                wu[rows, lanes] = stack(up).astype(BF)
            outs += [jnp.concatenate(out, 0), tails[rows, 16 * ctx : 16 * ctx + 16]]
        wo[rows, :] = jnp.concatenate(outs, 1).astype(BF)
        for i in range(8):
            at = pl.ds(pl.multiple_of(384 * x + 48 * i, 16), 48)
            wd[at, :] = jnp.concatenate(downs[i], 1).astype(BF)
        return carry

    lax.fori_loop(0, 4, block, 0)


def pack_wide(gg, gu, chunk, slots):
    zh, core = chunk // 2, chunk % 2

    def block(x, carry):
        rows = pl.ds(pl.multiple_of(144 * x, 16), 144)
        gate, up = gg[rows, :], gu[rows, :]
        for i in range(8):
            at = slice(18 * i, 18 * i + 18)
            slot = pack_rows(thin(gate[at], 3) + thin(up[at], 3), DOWN_AT).astype(BF)
            slots[core, x, i % 4, zh * 2 + i // 4, 0:DOWN_AT] = slot
        return carry

    lax.fori_loop(0, 4, block, 0)


def pack_down(gd, x, slots, tails):
    for ctx in range(4):
        zh, core = ctx // 2, ctx % 2
        for i in range(8):
            part = gd[48 * i : 48 * i + 48, 144 * ctx : 144 * ctx + 144]
            slots[core, x, i % 4, zh * 2 + i // 4, DOWN_AT:TAIL_AT] = part[:, :128].astype(BF)
            tails[x, i, ctx] = down_tail(part[:, 128:])


def pack_out(go, tails, slots):
    def block(x, carry):
        out = go[pl.ds(pl.multiple_of(144 * x, 16), 144), :]
        for ctx in range(4):
            zh, core = ctx // 2, ctx % 2
            main = out[:, 144 * ctx : 144 * ctx + 128]
            for i in range(8):
                pieces = [tails[x, i, ctx], main[18 * i : 18 * i + 18]]
                slot = pack_rows(pieces, LATE - TAIL_AT).astype(BF)
                slots[core, x, i % 4, zh * 2 + i // 4, TAIL_AT:LATE] = slot
        return carry

    lax.fori_loop(0, 4, block, 0)


def pack_early(gqkv, go, gains, out_ref):
    def block(x, carry):
        rows = pl.ds(pl.multiple_of(144 * x, 16), 144)
        whole = gqkv[rows, :]
        out = go[rows, :]
        for ctx in range(4):
            zh, core = ctx // 2, ctx % 2
            small = jnp.concatenate(
                [
                    whole[:, 144 * ctx : 144 * ctx + 144],
                    whole[:, D + 48 * ctx : D + 48 * ctx + 48],
                    whole[:, D + KV + 48 * ctx : D + KV + 48 * ctx + 48],
                    out[:, 144 * ctx + 128 : 144 * ctx + 144],
                ],
                1,
            )
            for i in range(8):
                pieces = thin(small[18 * i : 18 * i + 18], 2) + [gains[x, i]]
                slot = pack_rows(pieces, EARLY).astype(BF)
                out_ref[core, x, i % 4, zh * 2 + i // 4] = slot
        return carry

    lax.fori_loop(0, 4, block, 0)


def finish_kernel(early, late, out, dx, out_to, dx_to, ga, gm, gq, gk, gv, go, gg, gu, gd):
    def wide(slot, base, count):
        return jnp.concatenate(
            [slot[base + 18 * t : base + 18 * t + 18] for t in range(count)], 1
        )

    gg[...] = wide(late, 0, 3)
    gu[...] = wide(late, UP_AT, 3)
    gd[...] = jnp.concatenate([late[DOWN_AT:TAIL_AT], open_tail(late[TAIL_AT:OUT_AT])], 1)
    small = wide(early, 0, 2)
    gq[...] = small[:, :144]
    gk[...] = small[:, 144:192]
    gv[...] = small[:, 192:240]
    go[...] = jnp.concatenate([late[OUT_AT : OUT_AT + 18], small[:, 240:256]], 1)
    ga[...] = early[36:37, :18]
    gm[...] = early[37:38, :18]
    out_to[...] = out[...]
    dx_to[...] = dx[...]


def three_heads(ref, g, half, size):
    lanes = slice(half * size, half * size + size)
    base = g * GROUP * HEAD
    heads = [ref[base + HEAD * j : base + HEAD * j + HEAD, lanes] for j in range(GROUP)]
    return jnp.concatenate(heads, 1)


def turn(vectors, cosine, sine):
    first, second = vectors[: HEAD // 2], vectors[HEAD // 2 :]
    return jnp.concatenate([first * cosine - second * sine, second * cosine + first * sine], 0)


def columns_of(rows):
    full = jnp.concatenate([rows, jnp.zeros((2, 64), F32)], 1)
    turned = jnp.concatenate([full, jnp.zeros((126, 640), F32)], 0).T
    return turned[:D, 0:1], turned[:D, 1:2]


def rows_of(first, second):
    lane = lax.broadcasted_iota(jnp.int32, (D, 128), 1)
    full = jnp.where(lane == 0, first, jnp.where(lane == 1, second, 0.0))
    full = jnp.concatenate([full, jnp.zeros((64, 128), F32)], 0)
    return full.T[0:2, :D]


def causal(size):
    key = lax.broadcasted_iota(jnp.int32, (size, GROUP * size), 0)
    query = lax.broadcasted_iota(jnp.int32, (size, GROUP * size), 1) % size
    return key <= query


def mul(a, b, ca, cb):
    return lax.dot_general(a, b, (((ca,), (cb,)), ((), ())), preferred_element_type=F32)


class Context:
    def __init__(self, place, size):
        ctx = lax.axis_index("ctx")
        half, core = ctx // 2, ctx % 2
        self.size = size
        self.me = ctx
        self.sibling = half * 2 + 1 - core
        self.partner = (1 - half) * 2 + core
        self.corner = (1 - half) * 2 + 1 - core
        self.sibling_device = place.sibling()
        self.partner_device = place.peer(2, place.sides[2] // 2)

    def pairs(self, owner):
        late = jnp.where(owner > self.me, 1, 0)
        first, second = 1, late
        return (first, pl.ds(0, self.size)), (
            second,
            pl.ds(pl.multiple_of(late * self.size, self.size), self.size),
        )


def layer_kernel(sides, early_streams, late_gather, late_reduce, *refs):
    x_ref, dy_ref, wq, wk, wv, wo_ref, wg_ref, wu_ref, wd_ref = refs[:9]
    gain_a, gain_b, cos_ref, sin_ref = refs[9:13]
    out_ref, dx_ref, early_ref, total_ref = refs[13:17]
    scratch = refs[17:]
    early_slot, late_slot, early_slots, late_slots, kv_ref, kv_all = scratch[:6]
    queries, tops, totals, mixes, grads, lses, deltas, dqs = scratch[6:14]
    mixed_ref, normed_ref, wqkv, wo, wg, wu, wd, tails = scratch[14:22]
    middle, dmiddle, high, rising, falling, gate_grad, up_grad = scratch[22:29]
    out_grad, down_tails, acc, sent, passed, got, dqkv, gqkv, gain_rows = scratch[29:38]
    dy_rows = scratch[69]
    kv_sem, kv_send, kv_recv, back_send, back_recv = scratch[38:43]
    early_sems, late_sems = scratch[43:48], scratch[48:53]
    late_scratch, early_scratch = scratch[53:61], scratch[61:69]
    size = x_ref.shape[1] // 2
    place = Place(sides)
    ctx = Context(place, size)
    pack_weights(
        wq, wk, wv, wo_ref, wg_ref, wu_ref, wd_ref, (gain_a, gain_b), early_slot, late_slot
    )
    greet(place)
    early = Gather(place, early_streams, early_slot, early_slots, early_sems)
    gather = Gather(place, late_gather, late_slot, late_slots, late_sems)
    early.start()
    gather.start()

    def scale_of(values):
        return lax.rsqrt(jnp.mean(values * values, 0, keepdims=True) + 1e-05)

    inputs = x_ref[...].astype(F32)
    scale_one = scale_of(inputs)
    middle[...] = inputs * scale_one
    early.phase(1)
    gather.phase(1)
    early.phase(2)
    dy_rows[...] = dy_ref[...].astype(F32).T.astype(BF)
    for step in range(1, max(sides)):
        early.arrive(step)
    gather.phase(2)
    early.finish()
    unpack_early(early_slots, wqkv, tails)
    gain_one, gain_two = columns_of(unpack_gains(early_slots))
    normed_ref[...] = (middle[...] * gain_one).astype(BF)
    tables = [(cos_ref[b], sin_ref[b]) for b in (ctx.me, 7 - ctx.me)]
    pre = mul(wqkv[:, D:], normed_ref[...], 0, 0)
    for g in range(KV_HEADS):
        for half in range(2):
            lanes = slice(half * size, half * size + size)
            key = turn(pre[HEAD * g : HEAD * g + HEAD, lanes], *tables[half])
            both = jnp.concatenate([key, pre[KV + HEAD * g : KV + HEAD * g + HEAD, lanes]], 0)
            kv_ref[g, lanes, :] = both.T.astype(BF)
    far, near, corner = [], [], []
    for g in range(KV_HEADS):
        mine = kv_all.at[ctx.me, g]
        copy = remote(kv_ref.at[g], mine, kv_send.at[0, g], kv_recv.at[0, g], ctx.partner_device)
        copy.start()
        far.append(copy)
    for g in range(KV_HEADS):
        mine = kv_all.at[ctx.me, g]
        copy = remote(kv_ref.at[g], mine, kv_send.at[1, g], kv_recv.at[1, g], ctx.sibling_device)
        copy.start()
        near.append(copy)
    own = pltpu.make_async_copy(kv_ref, kv_all.at[ctx.me], kv_sem)
    own.start()
    for g in range(KV_HEADS):
        columns = slice(g * GROUP * HEAD, (g + 1) * GROUP * HEAD)
        pre = mul(wqkv[:, columns], normed_ref[...], 0, 0)
        for j in range(GROUP):
            for half in range(2):
                lanes = slice(half * size, half * size + size)
                turned = turn(pre[HEAD * j : HEAD * j + HEAD, lanes], *tables[half])
                turned = (turned * HEAD**-0.5).astype(BF)
                queries[g, half, :, size * j : size * j + size] = turned

    mask = causal(size)

    def scores_of(part):
        g, half, kv, masked = part[:4]
        scores = mul(kv[:, :HEAD], queries[g, half], 1, 0)
        return jnp.where(mask, scores, -1e30) if masked else scores

    def attend(parts):
        ahead = scores_of(parts[0])
        for n, (g, half, kv, masked, fresh) in enumerate(parts):
            scores = ahead
            if n + 1 < len(parts):
                ahead = scores_of(parts[n + 1])
            top = jnp.max(scores, 0, keepdims=True)
            if not fresh:
                before = tops[g, half]
                top = jnp.maximum(before, top)
            probs = jnp.exp(scores - top)
            total = jnp.sum(probs, 0, keepdims=True)
            mixed = mul(kv[:, HEAD:], probs.astype(BF), 0, 0)
            if not fresh:
                fade = jnp.exp(before - top)
                total += totals[g, half] * fade
                mixed += mixes[g, half] * fade
            tops[g, half], totals[g, half], mixes[g, half] = top, total, mixed

    def other(owner):
        parts = []
        for g in range(KV_HEADS):
            for half, rows in ctx.pairs(owner):
                parts.append((g, half, kv_all[owner, g, rows, :], False, False))
        attend(parts)

    parts = []
    for g in range(KV_HEADS):
        first, second = kv_ref[g, :size, :], kv_ref[g, size:, :]
        parts.append((g, 0, first, True, True))
        parts.append((g, 1, first, False, True))
        parts.append((g, 1, second, True, False))
    attend(parts)
    for copy in near:
        copy.wait_recv()
    other(ctx.sibling)
    for g in range(KV_HEADS):
        far[g].wait_recv()
        block = kv_all.at[ctx.partner, g]
        copy = remote(block, block, kv_send.at[2, g], kv_recv.at[2, g], ctx.sibling_device)
        copy.start()
        corner.append(copy)
    gather.arrive(1)
    other(ctx.partner)
    gather.arrive(2)
    for copy in corner:
        copy.wait_recv()
    own.wait()
    gather.arrive(3)
    other(ctx.corner)
    for g in range(KV_HEADS):
        for half in range(2):
            total = totals[g, half]
            mixed = (mixes[g, half] / total).astype(BF)
            lses[g, half] = tops[g, half] + jnp.log(total)
            lanes = slice(half * size, half * size + size)
            for j in range(GROUP):
                at = HEAD * (GROUP * g + j)
                mixed_ref[at : at + HEAD, lanes] = mixed[:, size * j : size * j + size]
    gather.finish()
    for copy in far + near + corner:
        copy.wait_send()

    unpack_late(late_slots, tails, wo, wg, wu, wd)
    middle[...] = x_ref[...].astype(F32) + mul(wo[...], mixed_ref[...], 0, 0)
    scale_two = scale_of(middle[...])
    normed_two = middle[...] * scale_two * gain_two
    high[...] = normed_two.astype(BF)
    low = normed_two.T.astype(BF)
    dy = dy_rows[...]
    rising[...] = jnp.zeros_like(rising)
    falling[...] = jnp.zeros_like(falling)

    def chunk(c, carry):
        lanes = pl.ds(pl.multiple_of(384 * c, 128), 384)
        gate_w, up_w, down_w = wg[:, lanes], wu[:, lanes], wd[lanes, :]
        gate = mul(low, gate_w, 1, 0)
        upper = mul(low, up_w, 1, 0)
        dhid = mul(dy, down_w, 1, 1)
        sigma = jax.nn.sigmoid(gate)
        silu = gate * sigma
        hidden = (silu * upper).astype(BF)
        dgate = (dhid * upper * sigma * (1.0 + gate * (1.0 - sigma))).astype(BF)
        dup = (dhid * silu).astype(BF)
        rising[...] += mul(hidden, down_w, 1, 0)
        falling[...] += mul(dgate, gate_w, 1, 1) + mul(dup, up_w, 1, 1)
        gate_grad[...] = mul(high[...], dgate, 1, 0)
        up_grad[...] = mul(high[...], dup, 1, 0)
        pack_wide(gate_grad, up_grad, c, late_slots)
        pack_down(mul(hidden, dy, 0, 0), c, late_slots, down_tails)
        return carry

    lax.fori_loop(0, 4, chunk, 0)
    out_ref[...] = (middle[...] + rising[...].T).astype(BF)
    grad = falling[...].T
    gain_grad_two = jnp.sum(grad * middle[...] * scale_two, 1, keepdims=True)
    gained = grad * gain_two
    dmiddle[...] = (
        dy_ref[...].astype(F32)
        + scale_two * gained
        - middle[...] * scale_two**3 * jnp.mean(middle[...] * gained, 0, keepdims=True)
    )
    dattn = dmiddle[...].astype(BF)
    out_grad[...] = mul(mixed_ref[...], dattn, 1, 1)
    pack_out(out_grad, down_tails, late_slots)
    reduce = Reduce(place, late_reduce, late_slots, total_ref, late_scratch)
    late_early = Reduce(place, early_streams, early_slots, early_ref, early_scratch)
    reduce.start()
    dmixed = mul(wo[...], dattn, 1, 0).astype(BF)
    for g in range(KV_HEADS):
        for half in range(2):
            grad = three_heads(dmixed, g, half, size)
            grads[g, half] = grad
            mixed = three_heads(mixed_ref, g, half, size)
            deltas[g, half] = jnp.sum(grad.astype(F32) * mixed.astype(F32), 0, keepdims=True)
    dqs[...] = jnp.zeros_like(dqs)

    def lead(part):
        g, half, kv, masked = part[:4]
        return scores_of(part), mul(kv[:, HEAD:], grads[g, half], 1, 0)

    def retrace(parts, give):
        ahead = lead(parts[0])
        for n, part in enumerate(parts):
            g, half, kv, masked = part
            scores, dprobs = ahead
            if n + 1 < len(parts):
                ahead = lead(parts[n + 1])
            probs = jnp.exp(scores - lses[g, half])
            dscores = (probs * (dprobs - deltas[g, half])).astype(BF)
            dvalue = mul(probs.astype(BF), grads[g, half], 1, 1)
            dkey = mul(dscores, queries[g, half], 1, 1)
            dqs[g, half] += mul(kv[:, :HEAD], dscores, 0, 0)
            give(n, g, jnp.concatenate([dkey, dvalue], 1))

    def back(owner, store):
        parts = []
        for g in range(KV_HEADS):
            for half, rows in ctx.pairs(owner):
                parts.append((g, half, kv_all[owner, g, rows, :], False))
        late = jnp.full((size, 128), owner, jnp.int32) > ctx.me
        kept = []

        def give(n, g, dkv):
            kept.append(dkv)
            if n % 2 == 1:
                store(g, kept[-2] + jnp.where(late, 0.0, dkv), jnp.where(late, dkv, 0.0))

        retrace(parts, give)

    def to_sibling(slot):
        def store(g, first, second):
            sent[slot, g, :size] = first.astype(BF)
            sent[slot, g, size:] = second.astype(BF)

        return store

    def to_acc(g, first, second):
        acc[g, :size] = first
        acc[g, size:] = second

    def send(slot):
        copies = []
        for g in range(KV_HEADS):
            copy = remote(
                sent.at[slot, g],
                got.at[slot, g],
                back_send.at[slot, g],
                back_recv.at[slot, g],
                ctx.sibling_device,
            )
            copy.start()
            copies.append(copy)
        return copies

    back(ctx.corner, to_sibling(0))
    copies = send(0)
    back(ctx.partner, to_acc)
    for copy in copies:
        copy.wait_recv()
    far = []
    for g in range(KV_HEADS):
        passed[g] = (acc[g] + got[0, g].astype(F32)).astype(BF)
        copy = remote(
            passed.at[g], got.at[2, g], back_send.at[2, g], back_recv.at[2, g], ctx.partner_device
        )
        copy.start()
        far.append(copy)
    reduce.phase_pair()
    back(ctx.sibling, to_sibling(1))
    near = send(1)
    parts, kept = [], []
    for g in range(KV_HEADS):
        first, second = kv_all[ctx.me, g, :size, :], kv_all[ctx.me, g, size:, :]
        parts += [(g, 0, first, True), (g, 1, first, False), (g, 1, second, True)]

    def keep(n, g, dkv):
        kept.append(dkv)
        if n % 3 == 2:
            to_acc(g, kept[-3] + kept[-2], dkv)

    retrace(parts, keep)
    for g in range(KV_HEADS):
        for half in range(2):
            lanes = slice(half * size, half * size + size)
            cosine, sine = tables[half]
            for j in range(GROUP):
                dquery = dqs[g, half, :, size * j : size * j + size] * HEAD**-0.5
                at = HEAD * (GROUP * g + j)
                dqkv[at : at + HEAD, lanes] = turn(dquery, cosine, -sine).astype(BF)
    for g in range(KV_HEADS):
        near[g].wait_recv()
        far[g].wait_recv()
        whole = (acc[g] + got[1, g].astype(F32) + got[2, g].astype(F32)).T
        at = D + HEAD * g
        for half in range(2):
            lanes = slice(half * size, half * size + size)
            cosine, sine = tables[half]
            dqkv[at : at + HEAD, lanes] = turn(whole[:HEAD, lanes], cosine, -sine).astype(BF)
        dqkv[at + KV : at + KV + HEAD, :] = whole[HEAD:].astype(BF)
    gqkv[...] = mul(normed_ref[...], dqkv[...], 1, 1)
    grad = mul(wqkv[...], dqkv[...], 1, 0)
    inputs = x_ref[...].astype(F32)
    scale_one = scale_of(inputs)
    gain_grad_one = jnp.sum(grad * inputs * scale_one, 1, keepdims=True)
    gain_grads = rows_of(gain_grad_one, gain_grad_two)
    for x in range(4):
        for i in range(8):
            at = 18 * (8 * x + i)
            gain_rows[x, i, :, 0:18] = gain_grads[:, at : at + 18]
    pack_early(gqkv, out_grad, gain_rows, early_slots)
    late_early.start()
    gained = grad * gain_one
    dx_ref[...] = (
        dmiddle[...]
        + scale_one * gained
        - inputs * scale_one**3 * jnp.mean(inputs * gained, 0, keepdims=True)
    )
    reduce.phase_first()
    late_early.phase_pair()
    reduce.phase_second()
    late_early.phase_first()
    late_early.phase_second()
    reduce.finish()
    late_early.finish()
    for copy in copies + far + near:
        copy.wait_send()


def layer(tokens, cotangent, weights, gains, sides):
    rows = tokens.shape[1]
    size = rows // 2
    vmem = pl.BlockSpec(memory_space=pltpu.VMEM)
    wide = GROUP * size
    kv = (KV_HEADS, rows, 2 * HEAD)
    heads = lambda height, kind: pltpu.VMEM((KV_HEADS, 2, height, wide), kind)
    dma = pltpu.SemaphoreType.DMA
    return pl.pallas_call(
        functools.partial(layer_kernel, sides, EARLY_STREAMS, LATE_GATHER, LATE_REDUCE),
        out_shape=[
            jax.ShapeDtypeStruct((D, rows), BF),
            jax.ShapeDtypeStruct((D, rows), F32),
            jax.ShapeDtypeStruct((EARLY, 128), F32),
            jax.ShapeDtypeStruct((LATE, 128), F32),
        ],
        in_specs=[vmem] * 13,
        out_specs=[vmem] * 4,
        scratch_shapes=[
            pltpu.VMEM((EARLY, 128), BF),
            pltpu.VMEM((LATE, 128), BF),
            pltpu.VMEM((2,) + sides + (EARLY, 128), BF),
            pltpu.VMEM((2,) + sides + (LATE, 128), BF),
            pltpu.VMEM(kv, BF),
            pltpu.VMEM((4,) + kv, BF),
            heads(HEAD, BF),
            heads(1, F32),
            heads(1, F32),
            heads(HEAD, F32),
            heads(HEAD, BF),
            heads(1, F32),
            heads(1, F32),
            heads(HEAD, F32),
            pltpu.VMEM((D, rows), BF),
            pltpu.VMEM((D, rows), BF),
            pltpu.VMEM((D, D + 2 * KV), BF),
            pltpu.VMEM((D, D), BF),
            pltpu.VMEM((D, FF), BF),
            pltpu.VMEM((D, FF), BF),
            pltpu.VMEM((FF, D), BF),
            pltpu.VMEM((D, 64), F32),
            pltpu.VMEM((D, rows), F32),
            pltpu.VMEM((D, rows), F32),
            pltpu.VMEM((D, rows), BF),
            pltpu.VMEM((rows, D), F32),
            pltpu.VMEM((rows, D), F32),
            pltpu.VMEM((D, FF // 4), F32),
            pltpu.VMEM((D, FF // 4), F32),
            pltpu.VMEM((D, D), F32),
            pltpu.VMEM((4, 8, 4, 8, 128), F32),
            pltpu.VMEM(kv, F32),
            pltpu.VMEM((2,) + kv, BF),
            pltpu.VMEM(kv, BF),
            pltpu.VMEM((3,) + kv, BF),
            pltpu.VMEM((D + 2 * KV, rows), BF),
            pltpu.VMEM((D, D + 2 * KV), F32),
            pltpu.VMEM((4, 8, 2, 128), F32),
            dma,
            dma((3, KV_HEADS)),
            dma((3, KV_HEADS)),
            dma((3, KV_HEADS)),
            dma((3, KV_HEADS)),
        ]
        + gather_sems(sides, EARLY_STREAMS)
        + gather_sems(sides, LATE_GATHER)
        + reduce_scratch(sides, LATE, LATE_REDUCE)
        + reduce_scratch(sides, EARLY, EARLY_STREAMS)
        + [pltpu.VMEM((rows, D), BF)],
        compiler_params=pltpu.CompilerParams(
            collective_id=0, has_side_effects=True, vmem_limit_bytes=VMEM_LIMIT
        ),
        name="decoder_layer",
    )(tokens, cotangent, *weights, *gains, *angles(size))


def angles(size):
    freq = 100000.0 ** (-np.arange(HEAD // 2) * 2.0 / HEAD)
    pos = np.arange(8 * size).reshape(8, 1, size)
    angle = pos * freq[None, :, None]
    return jnp.asarray(np.cos(angle), F32), jnp.asarray(np.sin(angle), F32)


def shards(
    tokens, cotangent, gain_attn, gain_mlp, w_query, w_key, w_value, w_out, w_gate, w_up, w_down
):
    sides = (4, 4, 4)
    result, grad_inputs, early_total, late_total = layer(
        tokens[0].T,
        cotangent[0].T,
        (w_query, w_key, w_value, w_out, w_gate, w_up, w_down),
        (gain_attn[None], gain_mlp[None]),
        sides,
    )
    shapes = [(1, 18), (1, 18), (18, 144), (18, 48), (18, 48), (18, 144), (18, 384), (18, 384)]
    out, dx, ga, gm, *grads = pl.pallas_call(
        finish_kernel,
        out_shape=[
            jax.ShapeDtypeStruct(result.shape, BF),
            jax.ShapeDtypeStruct(grad_inputs.shape, F32),
        ]
        + [jax.ShapeDtypeStruct(shape, F32) for shape in shapes + [(48, 144)]],
        name="finish",
    )(early_total, late_total, result, grad_inputs)
    return (out.T[None], dx.T[None], ga[0], gm[0], *grads)


def solution(mesh):
    both = P("dp", "ctx")
    block = P("dp", "ctx", None)
    return jax.shard_map(
        shards,
        mesh=mesh,
        in_specs=(block, block, P("dp"), P("dp")) + (both,) * 7,
        out_specs=(block, block, P("dp"), P("dp")) + (both,) * 7,
        check_vma=False,
    )
```

time: 1490 us -> 117 us (0.08)
  blocking collectives: 695 us -> 0 us
  waiting for transfers between devices: 384 us -> 0 us
  matrix products: 142 us -> 0 us
  Pallas kernels: 0 us -> 116 us
  local copies, waits for them, and re-layouts: 98.7 us -> 0 us
  starting transfers between devices: 84.4 us -> 0 us
  other arithmetic: 57.2 us -> 0 us
  between operations: 17 us -> 0.82 us
    all_gather x13 -> x0, blocking collectives: 399 us -> none  [the longest x1 83.2 us: shards(): lax.all_gather(columns[2], 'dp', axis=0, tiled=True)]
    unnamed x51 -> x0, waiting for transfers between devices: 301 us -> none
    unnamed x4 -> x0, blocking collectives: 296 us -> none
    dot_general x27 -> x0, matrix products: 142 us -> none  [the longest x1 28.9 us: shards(): jnp.einsum('qkgd,jkd->kgqj', grad_mixed, value_back, preferred_element_ty...]
    pallas_call x0 -> x2, Pallas kernels: none -> 116 us  [the longest x1 113 us: layer(): pl.pallas_call(functools.partial(layer_kernel, sides, EARLY_STREAMS, LATE...]
    unnamed x151 -> x0, local copies, waits for them, and re-layouts: 94.6 us -> none
    unnamed x38 -> x0, starting transfers between devices: 84.1 us -> none
    reduce_scatter x4 -> x0, waiting for transfers between devices: 82.4 us -> none  [the longest x1 29 us: shards(): lax.psum_scatter(summed[5], 'ctx', scatter_dimension=1, tiled=True)]
  transfers between devices with their start and end apart: 45 -> 0, of which waited for: 7 -> 0; matrix products, arithmetic and copies ran while one was open for 23% -> 0% of each run, Pallas kernels for 0% -> 0%
where the time goes in v1:
time: 117 us; the launch traced here: 116 us
  Pallas kernels  116 us (99%)
    pallas_call x1, Pallas kernels, layer(): pl.pallas_call(functools.partial(layer_kernel, sides, EARLY_STREAMS, LATE...  113 us
    pallas_call x1, Pallas kernels, shards(): pl.pallas_call(finish_kernel, out_shape=[jax.ShapeDtypeStruct(result.shap...  2.87 us

profile of v1, /device:TPU:0, one launch (start us, length us, event | category | flops | bytes accessed | tf_op | source)
XLA Modules:
  0.0 116.3 jit_solution(10541700410598270555)
XLA Ops:
  0.6 112.6 %decoder_layer.1 = (bf16[576,512]{1,0:T(8,128)(2,1)}, f32[576,512]{1,0:T(8,128)}, f32[48,128]{1,0:T(8,128)}, f32[192,128]{1,0:T(8,128)}) custom-call(bf16[576,512]{1,0:T(8,128)(2,1)} %bitcast.16, bf16[576,512]{1,0:T(8,128)(2,1)} %bitcast.17, bf16[18,144]{1,0:T(8,128)(2,1)} %refs_2_.1, bf16[18,48]{1,0:T(8,128)(2,1)} %refs_3_.1, bf16[18,48]{1,0:T(8,128)(2,1)} %refs_4_.1, ...), custom_call_target="tpu_custom_call" | custom-call | tf_op jit(solution)/shard_map/decoder_layer/pallas_call | solution.py:872
  113.3 2.9 %finish.1 = (bf16[576,512]{1,0:T(8,128)(2,1)}, f32[576,512]{1,0:T(8,128)}, f32[1,18]{1,0:T(1,128)}, f32[1,18]{1,0:T(1,128)}, f32[18,144]{1,0:T(8,128)}, /*index=...) custom-call(f32[48,128]{1,0:T(8,128)} %get-tuple-element.26.early, ...), custom_call_target="tpu_custom_call" | custom-call | tf_op jit(solution)/shard_map/finish/pallas_call | solution.py:958

commit v2 on v1

--- a/solution.py
+++ b/solution.py
@@ -173,20 +173,21 @@
         self.side = place.sides[0]
         self.sends = [[] for _ in streams]
 
+    def swap(self, index, at):
+        return remote(
+            self.grads_ref.at[(1 - self.place.core,) + at],
+            self.pair.at[at],
+            self.pair_send.at[index],
+            self.pair_recv.at[index],
+            self.place.sibling(),
+        )
+
     def start(self):
         self.swaps = []
-        core = self.place.core
         for number, (lo, hi, order) in enumerate(self.streams):
-            rows = pl.ds(lo, hi - lo)
-            copy = remote(
-                self.grads_ref.at[1 - core, :, :, :, rows],
-                self.pair.at[:, :, :, rows],
-                self.pair_send.at[number],
-                self.pair_recv.at[number],
-                self.place.sibling(),
-            )
+            copy = self.swap(number, (slice(None),) * 3 + (pl.ds(lo, hi - lo),))
             copy.start()
-            self.swaps.append(copy)
+            self.swaps.append([copy])
 
     def place_of(self, order, coords):
         index = [None, None, None]
@@ -218,7 +219,8 @@
         held, pair, side, core = self.grads_ref, self.pair, self.side, self.place.core
         for number, (lo, hi, order) in enumerate(self.streams):
             rows = pl.ds(lo, hi - lo)
-            self.swaps[number].wait_recv()
+            for copy in self.swaps[number]:
+                copy.wait_recv()
 
             def add(i, carry, rows=rows):
                 a, b = i // side, i % side
@@ -276,9 +278,7 @@
             for step in range(self.side - 1):
                 total += self.third[step, rows].astype(F32)
             self.out_ref[rows] = total
-        for copy in self.swaps:
-            copy.wait_send()
-        for group in self.sends:
+        for group in self.swaps + self.sends:
             for copy in group:
                 copy.wait_send()
 
@@ -290,8 +290,8 @@
         pltpu.VMEM((side - 1, side, side, rows, 128), BF),
         pltpu.VMEM((side - 1, side, rows, 128), BF),
         pltpu.VMEM((side - 1, rows, 128), BF),
-        pltpu.SemaphoreType.DMA((n,)),
-        pltpu.SemaphoreType.DMA((n,)),
+        pltpu.SemaphoreType.DMA((5,)),
+        pltpu.SemaphoreType.DMA((5,)),
         pltpu.SemaphoreType.DMA((n, 3, side - 1)),
         pltpu.SemaphoreType.DMA((n, 3, side - 1)),
     ]
@@ -391,16 +391,16 @@
     lax.fori_loop(0, 4, block, 0)
 
 
-def pack_wide(gg, gu, chunk, slots):
-    zh, core = chunk // 2, chunk % 2
-
+def pack_wide(gg, gu, zh, slots):
     def block(x, carry):
         rows = pl.ds(pl.multiple_of(144 * x, 16), 144)
-        gate, up = gg[rows, :], gu[rows, :]
-        for i in range(8):
-            at = slice(18 * i, 18 * i + 18)
-            slot = pack_rows(thin(gate[at], 3) + thin(up[at], 3), DOWN_AT).astype(BF)
-            slots[core, x, i % 4, zh * 2 + i // 4, 0:DOWN_AT] = slot
+        for core in range(2):
+            lanes = slice(384 * core, 384 * core + 384)
+            gate, up = gg[rows, lanes], gu[rows, lanes]
+            for i in range(8):
+                at = slice(18 * i, 18 * i + 18)
+                slot = pack_rows(thin(gate[at], 3) + thin(up[at], 3), DOWN_AT).astype(BF)
+                slots[core, x, i % 4, zh * 2 + i // 4, 0:DOWN_AT] = slot
         return carry
 
     lax.fori_loop(0, 4, block, 0)
@@ -685,8 +685,19 @@
     rising[...] = jnp.zeros_like(rising)
     falling[...] = jnp.zeros_like(falling)
 
+    reduce = Reduce(place, late_reduce, late_slots, total_ref, late_scratch)
+    every = slice(None)
+
+    def wide_swap(zh):
+        two = pl.ds(pl.multiple_of(2 * zh, 2), 2)
+        return reduce.swap(zh, (every, every, two, pl.ds(0, DOWN_AT)))
+
+    def down_swap(x):
+        two = pl.ds(pl.multiple_of(2 * x, 2), 2)
+        return reduce.swap(2 + x, (two, every, every, pl.ds(DOWN_AT, TAIL_AT - DOWN_AT)))
+
     def chunk(c, carry):
-        lanes = pl.ds(pl.multiple_of(384 * c, 128), 384)
+        lanes = pl.ds(pl.multiple_of(2 * 384 * c, 256), 2 * 384)
         gate_w, up_w, down_w = wg[:, lanes], wu[:, lanes], wd[lanes, :]
         gate = mul(low, gate_w, 1, 0)
         upper = mul(low, up_w, 1, 0)
@@ -701,10 +712,14 @@
         gate_grad[...] = mul(high[...], dgate, 1, 0)
         up_grad[...] = mul(high[...], dup, 1, 0)
         pack_wide(gate_grad, up_grad, c, late_slots)
-        pack_down(mul(hidden, dy, 0, 0), c, late_slots, down_tails)
+        wide_swap(c).start()
+        down_grad = mul(hidden, dy, 0, 0)
+        for k in range(2):
+            pack_down(down_grad[384 * k : 384 * k + 384], 2 * c + k, late_slots, down_tails)
+        down_swap(c).start()
         return carry
 
-    lax.fori_loop(0, 4, chunk, 0)
+    lax.fori_loop(0, 2, chunk, 0)
     out_ref[...] = (middle[...] + rising[...].T).astype(BF)
     grad = falling[...].T
     gain_grad_two = jnp.sum(grad * middle[...] * scale_two, 1, keepdims=True)
@@ -717,9 +732,11 @@
     dattn = dmiddle[...].astype(BF)
     out_grad[...] = mul(mixed_ref[...], dattn, 1, 1)
     pack_out(out_grad, down_tails, late_slots)
-    reduce = Reduce(place, late_reduce, late_slots, total_ref, late_scratch)
     late_early = Reduce(place, early_streams, early_slots, early_ref, early_scratch)
-    reduce.start()
+    tail_swap = reduce.swap(4, (every, every, every, pl.ds(TAIL_AT, LATE - TAIL_AT)))
+    tail_swap.start()
+    wides, downs = [wide_swap(0), wide_swap(1)], [down_swap(0), down_swap(1)]
+    reduce.swaps = [wides, downs, [tail_swap]]
     dmixed = mul(wo[...], dattn, 1, 0).astype(BF)
     for g in range(KV_HEADS):
         for half in range(2):
@@ -789,6 +806,7 @@
 
     back(ctx.corner, to_sibling(0))
     copies = send(0)
+    reduce.phase_pair()
     back(ctx.partner, to_acc)
     for copy in copies:
         copy.wait_recv()
@@ -800,7 +818,6 @@
         )
         copy.start()
         far.append(copy)
-    reduce.phase_pair()
     back(ctx.sibling, to_sibling(1))
     near = send(1)
     parts, kept = [], []
@@ -907,8 +924,8 @@
             pltpu.VMEM((D, rows), BF),
             pltpu.VMEM((rows, D), F32),
             pltpu.VMEM((rows, D), F32),
-            pltpu.VMEM((D, FF // 4), F32),
-            pltpu.VMEM((D, FF // 4), F32),
+            pltpu.VMEM((D, FF // 2), F32),
+            pltpu.VMEM((D, FF // 2), F32),
             pltpu.VMEM((D, D), F32),
             pltpu.VMEM((4, 8, 4, 8, 128), F32),
             pltpu.VMEM(kv, F32),

time: 117 us -> 115 us (0.983)
  Pallas kernels: 116 us -> 114 us
    pallas_call x1, Pallas kernels: 113 us -> 111 us  [layer(): pl.pallas_call(functools.partial(layer_kernel, sides, EARLY_STREAMS, LATE...]
where the time goes in v2:
time: 115 us
  Pallas kernels  114 us (99%)
    pallas_call x1, Pallas kernels, layer(): pl.pallas_call(functools.partial(layer_kernel, sides, EARLY_STREAMS, LATE...  111 us
    pallas_call x1, Pallas kernels, shards(): pl.pallas_call(finish_kernel, out_shape=[jax.ShapeDtypeStruct(result.shap...  2.87 us

profile of v2, /device:TPU:0, one launch (start us, length us, event | category | flops | bytes accessed | tf_op | source)
XLA Modules:
  0.0 115.0 jit_solution(9644851657322136242)
XLA Ops:
  0.6 111.3 %decoder_layer.1 = (bf16[576,512]{1,0:T(8,128)(2,1)}, f32[576,512]{1,0:T(8,128)}, f32[48,128]{1,0:T(8,128)}, f32[192,128]{1,0:T(8,128)}) custom-call(bf16[576,512]{1,0:T(8,128)(2,1)} %bitcast.16, bf16[576,512]{1,0:T(8,128)(2,1)} %bitcast.17, bf16[18,144]{1,0:T(8,128)(2,1)} %refs_2_.1, bf16[18,48]{1,0:T(8,128)(2,1)} %refs_3_.1, bf16[18,48]{1,0:T(8,128)(2,1)} %refs_4_.1, ...), custom_call_target="tpu_custom_call" | custom-call | tf_op jit(solution)/shard_map/decoder_layer/pallas_call | solution.py:889
  112.0 2.9 %finish.1 = (bf16[576,512]{1,0:T(8,128)(2,1)}, f32[576,512]{1,0:T(8,128)}, f32[1,18]{1,0:T(1,128)}, f32[1,18]{1,0:T(1,128)}, f32[18,144]{1,0:T(8,128)}, /*index=...) custom-call(f32[48,128]{1,0:T(8,128)} %get-tuple-element.26.early, ...), custom_call_target="tpu_custom_call" | custom-call | tf_op jit(solution)/shard_map/finish/pallas_call | solution.py:975

commit v3 on v2

--- a/solution.py
+++ b/solution.py
@@ -215,9 +215,10 @@
         for copy in self.sends[number][phase * (self.side - 1) : (phase + 1) * (self.side - 1)]:
             copy.wait_recv()
 
-    def phase_pair(self):
+    def phase_pair(self, numbers=(0, 1, 2)):
         held, pair, side, core = self.grads_ref, self.pair, self.side, self.place.core
-        for number, (lo, hi, order) in enumerate(self.streams):
+        for number in numbers:
+            lo, hi, order = self.streams[number]
             rows = pl.ds(lo, hi - lo)
             for copy in self.swaps[number]:
                 copy.wait_recv()
@@ -804,9 +805,10 @@
             copies.append(copy)
         return copies
 
+    reduce.phase_pair((0, 1))
     back(ctx.corner, to_sibling(0))
     copies = send(0)
-    reduce.phase_pair()
+    reduce.phase_pair((2,))
     back(ctx.partner, to_acc)
     for copy in copies:
         copy.wait_recv()

time: 115 us -> 115 us (level)
  no operation moved by 1% of the time
where the time goes in v3:
time: 115 us
  Pallas kernels  114 us (99%)
    pallas_call x1, Pallas kernels, layer(): pl.pallas_call(functools.partial(layer_kernel, sides, EARLY_STREAMS, LATE...  111 us
    pallas_call x1, Pallas kernels, shards(): pl.pallas_call(finish_kernel, out_shape=[jax.ShapeDtypeStruct(result.shap...  2.87 us

profile of v3, /device:TPU:0, one launch (start us, length us, event | category | flops | bytes accessed | tf_op | source)
XLA Modules:
  0.0 115.0 jit_solution(11877510600949810822)
XLA Ops:
  0.6 111.3 %decoder_layer.1 = (bf16[576,512]{1,0:T(8,128)(2,1)}, f32[576,512]{1,0:T(8,128)}, f32[48,128]{1,0:T(8,128)}, f32[192,128]{1,0:T(8,128)}) custom-call(bf16[576,512]{1,0:T(8,128)(2,1)} %bitcast.16, bf16[576,512]{1,0:T(8,128)(2,1)} %bitcast.17, bf16[18,144]{1,0:T(8,128)(2,1)} %refs_2_.1, bf16[18,48]{1,0:T(8,128)(2,1)} %refs_3_.1, bf16[18,48]{1,0:T(8,128)(2,1)} %refs_4_.1, ...), custom_call_target="tpu_custom_call" | custom-call | tf_op jit(solution)/shard_map/decoder_layer/pallas_call | solution.py:891
  112.0 2.9 %finish.1 = (bf16[576,512]{1,0:T(8,128)(2,1)}, f32[576,512]{1,0:T(8,128)}, f32[1,18]{1,0:T(1,128)}, f32[1,18]{1,0:T(1,128)}, f32[18,144]{1,0:T(8,128)}, /*index=...) custom-call(f32[48,128]{1,0:T(8,128)} %get-tuple-element.26.early, ...), custom_call_target="tpu_custom_call" | custom-call | tf_op jit(solution)/shard_map/finish/pallas_call | solution.py:977
